TPU v7x, 128 devices: a whole 4x4x4 slice. The times are simulated.
128 devices in a mesh: rep: 4 (over y), wide: 32 (over z, x, core).
Axes of the slice: x: 4, y: 4, z: 4, core: 2. Of those that a mesh axis runs over, the one named last changes fastest.
Arguments:
- amplitudes: bfloat16 [8, 32, 512, 2560], P(None, None, ('rep', 'wide')), may hold values from -6 to 6
- integrals: bfloat16 [8, 768, 81920], P(None, 'rep', 'wide'), may hold values from -0.01953125 to 0.01953125
- live_pairs: int32 [8], replicated, may hold values from 256 to 512, as said below
Outputs:
- ladder: bfloat16 [8, 512, 768], P(None, ('rep', 'wide'))
Inputs may be any that keep to these rules, and one draw needn't show every extreme that they name: `live_pairs`: rows of an irrep block at or beyond its count are padding; some irrep has all 512 pairs.
All inputs are finite; a program needn't handle non-finite values.
Results may differ from a plain program's by a relative error of at most 0.002.
Values may be sent and summed in bfloat16 or wider, within the bound.
A program may use at most 192 MiB of HBM per device.

v0:
```python
import jax
import jax.numpy as jnp
from jax import lax
from jax.sharding import PartitionSpec as P


def per_device(amplitudes, integrals, live_pairs):
    regrouped = lax.all_to_all(amplitudes, "wide", split_axis=1, concat_axis=1, tiled=True)
    irreps, members, owned, block = regrouped.shape
    partial_value = jnp.einsum(
        "gwsc,gac->gwsa",
        regrouped,
        lax.all_gather(integrals, "rep", axis=1, tiled=True),
        preferred_element_type=jnp.float32,
    )
    summed = lax.psum_scatter(partial_value, "wide", scatter_dimension=1, tiled=True)
    summed = summed.reshape(irreps, owned, summed.shape[3])
    local_rows = summed.shape[1]
    offset = lax.axis_index(("rep", "wide")) * local_rows
    index = offset + jnp.arange(local_rows, dtype=jnp.int32)
    keep = index[None, :] < live_pairs[:, None]
    return jnp.where(keep[:, :, None], summed, jnp.zeros_like(summed)).astype(jnp.bfloat16)


def solution(mesh):
    in_specs = (P(None, None, ("rep", "wide"), None), P(None, "rep", "wide"), P())
    out_specs = P(None, ("rep", "wide"), None)
    return jax.shard_map(
        per_device, mesh=mesh, in_specs=in_specs, out_specs=out_specs, check_vma=False
    )
```

profile of v0, /device:TPU:1, one launch (start us, length us, event | category | flops | bytes accessed | tf_op | source)
XLA Modules:
  0.0 402.4 jit_solution(8871119083709671757)
XLA Ops:
  6.5 0.0 all-gather.2.cloned.1.call-start
  6.5 0.7 all-gather.2.cloned.1.call-update
  7.3 0.0 reduce-scatter.2.cloned.1.call-start
  7.3 5.2 %copy.5 = bf16[8,32,4,2560]{3,2,0,1:T(4,128)(2,1)S(1)} copy(bf16[8,32,4,2560]{3,2,1,0:T(4,128)(2,1)} %param.3) | data formatting | bytes 10485760 | tf_op args[0]
  12.5 71.5 %all_to_all.5 = bf16[8,32,4,2560]{3,2,0,1:T(4,128)(2,1)} all-to-all(bf16[8,32,4,2560]{3,2,0,1:T(4,128)(2,1)S(1)} %copy.5), channel_id=1, replica_groups=mesh['rep'=4,'wide'=32] {'wide'}, dimensions={1} | all-to-all | bytes 10485760 | tf_op jit(solution)/shard_map/all_to_all | solution.py:8
  84.0 204.6 %all-gather.2.cloned.1.call-done = bf16[8,768,2560]{2,1,0:T(8,128)(2,1)} async-done(((bf16[8,192,2560]{2,1,0:T(8,128)(2,1)}), bf16[8,768,2560]{2,1,0:T(8,128)(2,1)}) %all-gather.2.cloned.1.call-update) | async-done | bytes 31457296 | tf_op jit(solution)/shard_map/all_gather | solution.py:13
  288.5 21.9 %fusion = f32[8,32,4,768]{3,1,2,0:T(8,128)S(1)} fusion(bf16[8,768,2560]{2,1,0:T(8,128)(2,1)} %all-gather.2.cloned.1.call-done, bf16[8,32,4,2560]{3,2,0,1:T(4,128)(2,1)} %all_to_all.5), kind=kOutput, calls=%fused_computation | convolution fusion | flops 4026531840 | bytes 39845888 | tf_op jit(solution)/shard_map/gwsc,gac->gwsa/dot_general | solution.py:10
  310.4 0.0 copy-start
  310.4 3.5 copy.7
  313.9 0.0 reduce-scatter.2.cloned.1.call-update
  314.0 0.0 copy-done
  314.0 0.1 broadcast_compare_fusion
  314.0 79.9 %reduce-scatter.2.cloned.1.call-done = f32[8,1,4,768]{3,0,2,1:T(8,128)} async-done(((f32[8,32,4,768]{3,0,2,1:T(8,128)}), f32[8,1,4,768]{3,0,2,1:T(8,128)}) %reduce-scatter.2.cloned.1.call-update) | async-done | bytes 98320 | tf_op jit(solution)/shard_map/reduce_scatter | solution.py:16
  393.9 1.0 fusion.3
  394.9 0.6 copy.8
  (1 shorter events, 0.0 us)
Async XLA Ops:
  6.5 282.0 %all-gather.2.cloned.1.call-start = ((), (), s32[]{:S(2)}) async-start(), calls=%async_computation.2 | async-start | bytes 39321600 | tf_op jit(solution)/shard_map/all_gather | solution.py:13
  7.3 386.7 %reduce-scatter.2.cloned.1.call-start = ((), (), s32[]{:S(2)}) async-start(), calls=%async_computation.3 | async-start | bytes 3244032 | tf_op jit(solution)/shard_map/reduce_scatter | solution.py:16
  310.4 3.5 copy-start
Sparse Core Ops, SparseCore 0:
  9.0 279.4 all-gather.1
  314.1 79.8 reduce-scatter.1
where the time goes:
time: 403 us; the launch traced here: 402 us
  waiting for transfers between devices  285 us (71%)
  blocking collectives  71.5 us (18%)
  matrix products  21.9 us (5%)
  between operations  13.4 us (3%)
  local copies, waits for them, and re-layouts  9.31 us (2%)
    all_gather x1, waiting for transfers between devices, per_device(): lax.all_gather(integrals, 'rep', axis=1, tiled=True)  205 us
    reduce_scatter x1, waiting for transfers between devices, per_device(): lax.psum_scatter(partial_value, 'wide', scatter_dimension=1, tiled=True)  79.9 us
    all_to_all x1, blocking collectives, per_device(): lax.all_to_all(amplitudes, 'wide', split_axis=1, concat_axis=1, tiled=True)  71.5 us
    dot_general x1, matrix products, per_device(): jnp.einsum('gwsc,gac->gwsa', regrouped, lax.all_gather(integrals, 'rep',...  21.9 us
  transfers between devices with their start and end apart: 2, of which 2 were waited for; matrix products, arithmetic and copies ran while one was open for 1% of the time, Pallas kernels for 0%

commit v1 on v0

v1 whole, which is shorter than its diff:
```python
import functools

import jax
import jax.numpy as jnp
from jax import lax
from jax.experimental import pallas as pl
from jax.experimental.pallas import tpu as pltpu
from jax.sharding import PartitionSpec as P

MESH = pl.DeviceIdType.MESH
MIB = 2**20


def ladder_kernel(reps, members, amp, integ, out, rows, relay, cols, part, landed, summed, placed,
                  b_send, b_recv, b_own, a_send, a_recv, y_send, y_recv, r_send, r_recv, o_send, o_recv):
    r, w = lax.axis_index("rep"), lax.axis_index("wide")
    up, down, across = (r + 1) % reps, (r + reps - 1) % reps, (r + 2) % reps
    cuts = integ.shape[1]
    owned = amp.shape[2]
    halves = amp.shape[0] // reps

    def irrep(behind, half):
        return (r + reps - behind) % reps + reps * half

    def remote(src, dst, send, recv, rep, member):
        return pltpu.make_async_remote_copy(
            src_ref=src, dst_ref=dst, send_sem=send, recv_sem=recv, device_id=(rep, member), device_id_type=MESH
        )

    def wait_for(ref, sem):
        pltpu.make_async_copy(ref, ref, sem).wait()

    def other(t):
        return (w + t) % members

    barrier = pltpu.get_barrier_semaphore()
    for rep in (up, down, across):
        pl.semaphore_signal(barrier, inc=1, device_id=(rep, w), device_id_type=MESH)

    def greet(t, carry):
        pl.semaphore_signal(barrier, inc=1, device_id=(r, other(t)), device_id_type=MESH)
        return carry

    lax.fori_loop(1, members, greet, 0)
    pl.semaphore_wait(barrier, members + 2)

    mine, theirs = pl.ds(0, cuts), pl.ds(cuts, cuts)

    def send_columns(half):
        remote(integ.at[irrep(3, half)], cols.at[half, 0, theirs], b_send.at[half, 0], b_recv.at[half, 0], up, w).start()
        remote(integ.at[irrep(2, half)], cols.at[half, 1, theirs], b_send.at[half, 1], b_recv.at[half, 1], down, w).start()

    def own_columns(half, role):
        return pltpu.make_async_copy(integ.at[irrep(role, half)], cols.at[half, role, mine], b_own.at[half, role])

    def arriving(behind, half):
        return rows.at[half, behind, 0] if behind < 2 else relay.at[half, behind - 2]

    def spread(behind, half):
        g, target = irrep(behind, half), arriving(behind, half)
        send, recv = a_send.at[half, behind], a_recv.at[half, behind]
        pltpu.make_async_copy(amp.at[g, w], target.at[w], recv).start()

        def one(t, carry):
            remote(amp.at[g, other(t)], target.at[w], send, recv, r, other(t)).start()
            return carry

        lax.fori_loop(1, members, one, 0)

    def arrived(behind, half):
        wait_for(arriving(behind, half), a_recv.at[half, behind])

    def along(src, half, role, slot, rep, index):
        return remote(src, rows.at[half, role, slot], y_send.at[half, index], y_recv.at[half, role, slot - 1], rep, w)

    def relay_rows(half):
        arrived(3, half)
        along(relay.at[half, 1], half, 0, 2, up, 0).start()
        arrived(2, half)
        along(relay.at[half, 0], half, 1, 2, down, 1).start()

    def exchange_rows(half):
        arrived(0, half)
        along(rows.at[half, 0, 0], half, 1, 1, up, 2).start()
        arrived(1, half)
        along(rows.at[half, 1, 0], half, 0, 1, down, 3).start()

    def took(half, role, slot):
        wait_for(rows.at[half, role, slot], y_recv.at[half, role, slot - 1])

    def forward_rows(half):
        took(half, 0, 2)
        along(rows.at[half, 0, 2], half, 1, 3, up, 4).start()
        took(half, 1, 2)
        along(rows.at[half, 1, 2], half, 0, 3, down, 5).start()

    def multiply(half, role, slot):
        left = rows[half, role, slot].reshape(members * owned, rows.shape[-1])
        product = lax.dot_general(
            left, cols[half, role], (((1,), (1,)), ((), ())), preferred_element_type=jnp.float32
        )
        part[half, role, :, slot] = product.reshape(members, owned, 2 * cuts)

    def give(half, role, slots, stage):
        send, recv = r_send.at[half, role, stage], r_recv.at[half, role, stage]
        pltpu.make_async_copy(part.at[half, role, w, slots], landed.at[half, role, w, slots], recv).start()

        def one(t, carry):
            remote(
                part.at[half, role, other(t), slots], landed.at[half, role, w, slots], send, recv, r, other(t)
            ).start()
            return carry

        lax.fori_loop(1, members, one, 0)

    def add_up(half, role, slots, stage):
        wait_for(landed.at[half, role, :, slots], r_recv.at[half, role, stage])
        summed[half, role, slots] = jnp.sum(landed[half, role, :, slots], axis=0)

    def hand_out(half, role, slots):
        g = irrep(role, half)
        place = {0: r, 1: (up, down)[role], 2: (down, up)[role], 3: across}
        for slot in slots:
            if slot == 0:
                placed[g, role] = summed[half, role, 0]
            else:
                remote(summed.at[half, role, slot], placed.at[g, role], o_send.at[half, role, slot - 1],
                       o_recv.at[half], place[slot], w).start()

    every, early, late = pl.ds(0, 4), pl.ds(0, 3), pl.ds(3, 1)

    send_columns(0)
    spread(3, 0)
    spread(2, 0)
    for half in range(halves):
        for role in range(2):
            own_columns(half, role).start()
    spread(0, 0)
    spread(1, 0)
    relay_rows(0)
    exchange_rows(0)
    send_columns(1)
    spread(3, 1)
    spread(2, 1)
    forward_rows(0)
    spread(0, 1)
    spread(1, 1)
    relay_rows(1)
    exchange_rows(1)

    def columns_ready(half, role):
        own_columns(half, role).wait()
        wait_for(cols.at[half, role, theirs], b_recv.at[half, role])

    for role in range(2):
        columns_ready(0, role)
        multiply(0, role, 0)
        multiply(0, role, 2)
        took(0, role, 1)
        multiply(0, role, 1)
    for role in range(2):
        took(0, role, 3)
        multiply(0, role, 3)
        give(0, role, every, 0)
    forward_rows(1)
    for role in range(2):
        columns_ready(1, role)
        multiply(1, role, 0)
        multiply(1, role, 2)
    for role in range(2):
        add_up(0, role, every, 0)
        hand_out(0, role, range(4))
    for role in range(2):
        took(1, role, 1)
        multiply(1, role, 1)
        give(1, role, early, 0)
    for role in range(2):
        add_up(1, role, early, 0)
        hand_out(1, role, range(3))
    for role in range(2):
        took(1, role, 3)
        multiply(1, role, 3)
        give(1, role, late, 1)
    for role in range(2):
        add_up(1, role, late, 1)
        hand_out(1, role, (3,))

    for half in range(halves):
        wait_for(placed.at[pl.ds(reps * half, reps - 1)], o_recv.at[half])
    out[...] = placed[...]

    for half in range(halves):
        for role in range(2):
            wait_for(cols.at[half, role, theirs], b_send.at[half, role])
            for slot in range(3):
                wait_for(summed.at[half, role, slot], o_send.at[half, role, slot])
        for behind in range(reps):
            wait_for(relay.at[half, 0, pl.ds(1, members - 1)], a_send.at[half, behind])
        for index in range(6):
            wait_for(rows.at[half, 0, 0], y_send.at[half, index])
    some = pl.ds(1, members - 1)
    for role in range(2):
        wait_for(landed.at[0, role, some, every], r_send.at[0, role, 0])
        wait_for(landed.at[1, role, some, early], r_send.at[1, role, 0])
        wait_for(landed.at[1, role, some, late], r_send.at[1, role, 1])


def per_device(reps, members, amplitudes, integrals, live_pairs):
    irreps, blocks, owned, depth = amplitudes.shape
    cuts = integrals.shape[1]
    halves = irreps // reps
    dma = pltpu.SemaphoreType.DMA
    f32, bf16 = jnp.float32, jnp.bfloat16
    pieces = pl.pallas_call(
        functools.partial(ladder_kernel, reps, members),
        out_shape=jax.ShapeDtypeStruct((irreps, 2, owned, 2 * cuts), f32),
        in_specs=[pl.BlockSpec(memory_space=pl.ANY)] * 2,
        out_specs=pl.BlockSpec(memory_space=pltpu.VMEM),
        scratch_shapes=[
            pltpu.VMEM((halves, 2, 4, members, owned, depth), bf16),
            pltpu.VMEM((halves, 2, members, owned, depth), bf16),
            pltpu.VMEM((halves, 2, 2 * cuts, depth), bf16),
            pltpu.VMEM((halves, 2, members, 4, owned, 2 * cuts), f32),
            pltpu.VMEM((halves, 2, members, 4, owned, 2 * cuts), f32),
            pltpu.VMEM((halves, 2, 4, owned, 2 * cuts), f32),
            pltpu.VMEM((irreps, 2, owned, 2 * cuts), f32),
            dma((halves, 2)), dma((halves, 2)), dma((halves, 2)),
            dma((halves, 4)), dma((halves, 4)),
            dma((halves, 6)), dma((halves, 2, 3)),
            dma((halves, 2, 2)), dma((halves, 2, 2)),
            dma((halves, 2, 3)), dma((halves,)),
        ],
        compiler_params=pltpu.CompilerParams(collective_id=0, has_side_effects=True, vmem_limit_bytes=52 * MIB),
        cost_estimate=pl.CostEstimate(
            flops=2 * irreps * owned * members * 4 * cuts * depth, bytes_accessed=26 * MIB, transcendentals=0
        ),
        name="ladder",
    )(amplitudes, integrals)

    quarters = []
    for g in range(irreps):
        found = {}
        for role in range(2):
            here = (g + role) % reps
            found[here] = pieces[g, role, :, :cuts]
            found[(here + (reps - 1, 1)[role]) % reps] = pieces[g, role, :, cuts:]
        quarters.append(jnp.concatenate([found[q] for q in range(reps)], axis=1))
    ladder = jnp.stack(quarters)
    index = (lax.axis_index("rep") * members + lax.axis_index("wide")) * owned + jnp.arange(owned, dtype=jnp.int32)
    keep = index[None, :] < live_pairs[:, None]
    return jnp.where(keep[:, :, None], ladder, jnp.zeros_like(ladder)).astype(jnp.bfloat16)


def solution(mesh):
    in_specs = (P(None, None, ("rep", "wide"), None), P(None, "rep", "wide"), P())
    out_specs = P(None, ("rep", "wide"), None)
    return jax.shard_map(
        functools.partial(per_device, mesh.shape["rep"], mesh.shape["wide"]),
        mesh=mesh, in_specs=in_specs, out_specs=out_specs, check_vma=False,
    )
```

time: 403 us -> 154 us (0.38)
  waiting for transfers between devices: 285 us -> 0 us
  Pallas kernels: 0 us -> 152 us
  blocking collectives: 71.5 us -> 0 us
  matrix products: 21.9 us -> 0 us
  between operations: 13.4 us -> 0.02 us
  local copies, waits for them, and re-layouts: 9.31 us -> 0.17 us
    all_gather x1 -> x0, waiting for transfers between devices: 205 us -> none  [per_device(): lax.all_gather(integrals, 'rep', axis=1, tiled=True)]
    pallas_call x0 -> x1, Pallas kernels: none -> 152 us  [per_device(): pl.pallas_call(functools.partial(ladder_kernel, reps, members), out_shape...]
    reduce_scatter x1 -> x0, waiting for transfers between devices: 79.9 us -> none  [per_device(): lax.psum_scatter(partial_value, 'wide', scatter_dimension=1, tiled=True)]
    all_to_all x1 -> x0, blocking collectives: 71.5 us -> none  [per_device(): lax.all_to_all(amplitudes, 'wide', split_axis=1, concat_axis=1, tiled=True)]
    dot_general x1 -> x0, matrix products: 21.9 us -> none  [per_device(): jnp.einsum('gwsc,gac->gwsa', regrouped, lax.all_gather(integrals, 'rep',...]
    unnamed x3 -> x0, local copies, waits for them, and re-layouts: 5.21 us -> none
  transfers between devices with their start and end apart: 2 -> 0, of which waited for: 2 -> 0; matrix products, arithmetic and copies ran while one was open for 1% -> 0% of each run, Pallas kernels for 0% -> 0%
where the time goes in v1:
time: 154 us
  Pallas kernels  152 us (99%)
  other arithmetic  2.11 us (1%)
    pallas_call x1, Pallas kernels, per_device(): pl.pallas_call(functools.partial(ladder_kernel, reps, members), out_shape...  152 us

profile of v1, /device:TPU:1, one launch (start us, length us, event | category | flops | bytes accessed | tf_op | source)
XLA Modules:
  0.0 154.0 jit_solution(12647512548400057306)
XLA Ops:
  0.0 0.7 broadcast_compare_fusion
  0.7 151.7 %ladder.1 = f32[8,2,4,384]{3,2,1,0:T(4,128)S(1)} custom-call(bf16[8,32,4,2560]{3,2,1,0:T(4,128)(2,1)} %amp.1, bf16[8,192,2560]{2,1,0:T(8,128)(2,1)} %integ.1), custom_call_target="tpu_custom_call" | custom-call | flops 4026531840 | bytes 27262976 | tf_op jit(solution)/shard_map/ladder/pallas_call | solution.py:214
  152.5 0.1 slice_bitcast_fusion.19
  152.6 0.1 slice_bitcast_fusion.3
  152.6 0.1 constant_dynamic-update-slice_fusion.7
  152.7 0.1 constant_dynamic-update-slice_fusion.6
  152.8 0.1 constant_dynamic-update-slice_fusion.5
  152.9 0.1 constant_dynamic-update-slice_fusion.4
  153.0 0.1 constant_dynamic-update-slice_fusion.3
  153.1 0.1 constant_dynamic-update-slice_fusion.2
  153.1 0.1 constant_dynamic-update-slice_fusion.1
  153.2 0.1 constant_dynamic-update-slice_fusion
  153.3 0.7 select_convert_fusion
  (1 shorter events, 0.0 us)

commit v2 on v1

v2 whole, which is shorter than its diff:
```python
import functools

import jax
import jax.numpy as jnp
from jax import lax
from jax.experimental import pallas as pl
from jax.experimental.pallas import tpu as pltpu
from jax.sharding import PartitionSpec as P

MESH = pl.DeviceIdType.MESH
MIB = 2**20
GROUP = 8


def ladder_kernel(reps, members, live, amp, integ, out, rows, relay, cols, part, landed, summed, placed, direct,
                  b_send, b_recv, b_own, a_send, a_recv, y_send, y_recv, p_send, p_recv,
                  r_send, r_recv, l_send, l_recv, o_send, o_recv, d_send, d_recv):
    r, w = lax.axis_index("rep"), lax.axis_index("wide")
    up, down, across = (r + 1) % reps, (r + reps - 1) % reps, (r + 2) % reps
    groups = members // GROUP
    plane, seat = w // GROUP, w % GROUP
    cuts = integ.shape[1]
    owned, depth = amp.shape[2], amp.shape[3]
    halves = amp.shape[0] // reps
    beside = {1: (down, up), 2: (across, across), 3: (up, down)}

    def irrep(behind, half):
        return (r + reps - behind) % reps + reps * half

    def remote(src, dst, send, recv, rep, member):
        return pltpu.make_async_remote_copy(
            src_ref=src, dst_ref=dst, send_sem=send, recv_sem=recv, device_id=(rep, member), device_id_type=MESH
        )

    def wait_for(ref, sem):
        pltpu.make_async_copy(ref, ref, sem).wait()

    def other(t):
        return (w + t) % members

    def neighbour(t):
        return plane * GROUP + (seat + t) % GROUP

    barrier = pltpu.get_barrier_semaphore()

    def greet(rep, member):
        pl.semaphore_signal(barrier, inc=1, device_id=(rep, member), device_id_type=MESH)

    def greet_rep(t, carry):
        greet(r, other(t))
        return carry

    def greet_group(t, carry):
        greet(up, neighbour(t))
        greet(down, neighbour(t))
        return carry

    greet(across, w)
    lax.fori_loop(0, GROUP, greet_group, 0)
    lax.fori_loop(1, members, greet_rep, 0)
    pl.semaphore_wait(barrier, members + 2 * GROUP)

    mine, theirs = pl.ds(0, cuts), pl.ds(cuts, cuts)

    def send_columns(half):
        remote(integ.at[irrep(3, half)], cols.at[half, 0, theirs], b_send.at[half, 0], b_recv.at[half, 0], up, w).start()
        remote(integ.at[irrep(2, half)], cols.at[half, 1, theirs], b_send.at[half, 1], b_recv.at[half, 1], down, w).start()

    def own_columns(half, role):
        return pltpu.make_async_copy(integ.at[irrep(role, half)], cols.at[half, role, mine], b_own.at[half, role])

    def columns_ready(half):
        for role in range(2):
            own_columns(half, role).wait()
            wait_for(cols.at[half, role, theirs], b_recv.at[half, role])

    def arriving(behind, half):
        return rows.at[half, behind, 0] if behind < 2 else relay.at[half, behind - 2]

    def spread(behind, half):
        g, target = irrep(behind, half), arriving(behind, half)
        send, recv = a_send.at[half, behind], a_recv.at[half, behind]
        pltpu.make_async_copy(amp.at[g, w], target.at[w], recv).start()

        def one(t, carry):
            remote(amp.at[g, other(t)], target.at[w], send, recv, r, other(t)).start()
            return carry

        lax.fori_loop(1, members, one, 0)

    def arrived(behind, half):
        wait_for(arriving(behind, half), a_recv.at[half, behind])

    def along(src, half, role, slot, rep):
        return remote(src, rows.at[half, role, slot], y_send.at[half, role, slot - 1], y_recv.at[half, role, slot - 1],
                      rep, w)

    def relay_rows(half):
        arrived(3, half)
        along(relay.at[half, 1], half, 0, 1, up).start()
        arrived(2, half)
        along(relay.at[half, 0], half, 1, 1, down).start()

    def forward_rows(half):
        took(half, 0, 1)
        along(rows.at[half, 0, 1], half, 1, 2, up).start()
        took(half, 1, 1)
        along(rows.at[half, 1, 1], half, 0, 2, down).start()

    def exchange_rows(half):
        arrived(0, half)
        along(rows.at[half, 0, 0], half, 1, 3, up).start()
        arrived(1, half)
        along(rows.at[half, 1, 0], half, 0, 3, down).start()

    def took(half, role, slot):
        wait_for(rows.at[half, role, slot], y_recv.at[half, role, slot - 1])

    def sent(half, slot):
        for role in range(2):
            wait_for(rows.at[half, role, slot], y_send.at[half, role, slot - 1])

    def group_at(step):
        return pl.ds((plane + step) % groups * GROUP, GROUP)

    def exchange_piece(step):
        for role, rep in ((0, up), (1, down)):
            remote(rows.at[1, role, 0, group_at(step)], rows.at[1, 1 - role, 3, group_at(step)],
                   p_send.at[role, step], p_recv.at[1 - role, step], rep, w).start()

    def product(left, half, role):
        return lax.dot_general(left, cols[half, role], (((1,), (1,)), ((), ())), preferred_element_type=jnp.float32)

    def multiply(half, role, slot):
        left = rows[half, role, slot].reshape(members * owned, depth)
        part[half, role, :, slot] = product(left, half, role).reshape(members, owned, 2 * cuts)

    def multiply_piece(step):
        for role in range(2):
            at = group_at(step)
            wait_for(rows.at[1, role, 3, at], p_recv.at[role, step])
            left = rows[1, role, 3, at].reshape(GROUP * owned, depth)
            part[1, role, at, 3] = product(left, 1, role).reshape(GROUP, owned, 2 * cuts)

    def give(half, role, slots):
        send, recv = r_send.at[half, role], r_recv.at[half, role]
        pltpu.make_async_copy(part.at[half, role, w, slots], landed.at[half, role, w, slots], recv).start()

        def one(t, carry):
            remote(
                part.at[half, role, other(t), slots], landed.at[half, role, w, slots], send, recv, r, other(t)
            ).start()
            return carry

        lax.fori_loop(1, members, one, 0)

    def give_piece(step):
        base = (plane + step) % groups * GROUP

        def one(t, carry):
            member = base + (seat + t) % GROUP
            remote(part.at[1, :, member, 3], landed.at[1, :, step * GROUP + seat, 3], l_send, l_recv, r, member).start()
            return carry

        lax.fori_loop(0, GROUP, one, 0)

    def give_direct():
        def one(t, carry):
            for role in range(2):
                remote(part.at[1, role, neighbour(t), 3], direct.at[role, seat], d_send, d_recv,
                       beside[3][role], neighbour(t)).start()
            return carry

        lax.fori_loop(0, GROUP, one, 0)

    def add_up(half, role, slots):
        wait_for(landed.at[half, role, :, slots], r_recv.at[half, role])
        summed[half, role, slots] = jnp.sum(landed[half, role, :, slots], axis=0)

    far = pl.ds(GROUP, members - GROUP)

    def add_up_pieces():
        wait_for(landed.at[1, :, far, 3], l_recv)
        summed[1, :, 3] = jnp.sum(landed[1, :, far, 3], axis=1)

    def hand_out(half, role, slots):
        g = irrep(role, half)
        for slot in slots:
            if slot == 0:
                placed[g, role] = summed[half, role, 0]
            else:
                remote(summed.at[half, role, slot], placed.at[g, role], o_send.at[half, role, slot - 1],
                       o_recv.at[half], beside[slot][role], w).start()

    def finish(half):
        index = (r * members + w) * owned + lax.broadcasted_iota(jnp.int32, (owned, reps * cuts), 0)
        for p in range(reps):
            g = reps * half + p
            found = {}
            for role, beyond in ((0, reps - 1), (1, 1)):
                here = (p + role) % reps
                found[here] = placed[g, role, :, :cuts]
                found[(here + beyond) % reps] = placed[g, role, :, cuts:]
            ladder = jnp.concatenate([found[q] for q in range(reps)], axis=1)
            out[g] = jnp.where(index < live[g], ladder, 0.0).astype(out.dtype)

    every, early = pl.ds(0, 4), pl.ds(0, 3)

    send_columns(0)
    spread(3, 0)
    spread(2, 0)
    for half in range(halves):
        for role in range(2):
            own_columns(half, role).start()
    spread(3, 1)
    spread(2, 1)
    relay_rows(0)
    relay_rows(1)
    send_columns(1)
    spread(0, 0)
    spread(1, 0)
    spread(0, 1)
    spread(1, 1)
    forward_rows(0)
    exchange_rows(0)
    forward_rows(1)

    columns_ready(0)
    for role in range(2):
        multiply(0, role, 0)
        multiply(0, role, 1)
    for role in range(2):
        took(0, role, 2)
        multiply(0, role, 2)
    arrived(0, 1)
    arrived(1, 1)
    columns_ready(1)
    for role in range(2):
        multiply(1, role, 0)
        multiply(1, role, 1)
    sent(0, 3)
    exchange_piece(1)
    exchange_piece(2)
    for role in range(2):
        took(0, role, 3)
        multiply(0, role, 3)
        give(0, role, every)
    for role in range(2):
        add_up(0, role, every)
        hand_out(0, role, range(4))
    sent(1, 2)
    exchange_piece(3)
    exchange_piece(0)
    for role in range(2):
        took(1, role, 2)
        multiply(1, role, 2)
        give(1, role, early)
    multiply_piece(1)
    give_piece(1)
    for role in range(2):
        add_up(1, role, early)
        hand_out(1, role, range(3))
    multiply_piece(2)
    give_piece(2)
    wait_for(placed.at[pl.ds(0, reps - 1)], o_recv.at[0])
    finish(0)
    multiply_piece(3)
    give_piece(3)
    multiply_piece(0)
    give_direct()
    add_up_pieces()
    for role in range(2):
        hand_out(1, role, (3,))
    wait_for(direct, d_recv)
    wait_for(placed.at[pl.ds(reps, reps - 1)], o_recv.at[1])
    for role, behind in ((0, 1), (1, 0)):
        g = irrep(behind, 1)
        placed[g, role] = placed[g, role] + jnp.sum(direct[role], axis=0)
    finish(1)

    for half in range(halves):
        for role in range(2):
            wait_for(cols.at[half, role, theirs], b_send.at[half, role])
            for slot in range(3):
                wait_for(summed.at[half, role, slot], o_send.at[half, role, slot])
        for behind in range(reps):
            wait_for(relay.at[half, 0, pl.ds(1, members - 1)], a_send.at[half, behind])
        sent(half, 1)
    sent(0, 2)
    some = pl.ds(1, members - 1)
    for role in range(2):
        for step in range(groups):
            wait_for(rows.at[1, role, 0, group_at(step)], p_send.at[role, step])
        wait_for(landed.at[0, role, some, every], r_send.at[0, role])
        wait_for(landed.at[1, role, some, early], r_send.at[1, role])
    wait_for(landed.at[1, :, far, 3], l_send)
    wait_for(direct, d_send)


def per_device(reps, members, amplitudes, integrals, live_pairs):
    irreps, blocks, owned, depth = amplitudes.shape
    cuts = integrals.shape[1]
    halves = irreps // reps
    dma = pltpu.SemaphoreType.DMA
    f32, bf16 = jnp.float32, jnp.bfloat16
    return pl.pallas_call(
        functools.partial(ladder_kernel, reps, members),
        out_shape=jax.ShapeDtypeStruct((irreps, owned, reps * cuts), bf16),
        in_specs=[pl.BlockSpec(memory_space=pltpu.SMEM)] + [pl.BlockSpec(memory_space=pl.ANY)] * 2,
        out_specs=pl.BlockSpec(memory_space=pltpu.VMEM),
        scratch_shapes=[
            pltpu.VMEM((halves, 2, 4, members, owned, depth), bf16),
            pltpu.VMEM((halves, 2, members, owned, depth), bf16),
            pltpu.VMEM((halves, 2, 2 * cuts, depth), bf16),
            pltpu.VMEM((halves, 2, members, 4, owned, 2 * cuts), f32),
            pltpu.VMEM((halves, 2, members, 4, owned, 2 * cuts), f32),
            pltpu.VMEM((halves, 2, 4, owned, 2 * cuts), f32),
            pltpu.VMEM((irreps, 2, owned, 2 * cuts), f32),
            pltpu.VMEM((2, GROUP, owned, 2 * cuts), f32),
            dma((halves, 2)), dma((halves, 2)), dma((halves, 2)),
            dma((halves, 4)), dma((halves, 4)),
            dma((halves, 2, 3)), dma((halves, 2, 3)),
            dma((2, 4)), dma((2, 4)),
            dma((halves, 2)), dma((halves, 2)),
            dma, dma,
            dma((halves, 2, 3)), dma((halves,)),
            dma, dma,
        ],
        compiler_params=pltpu.CompilerParams(collective_id=0, has_side_effects=True, vmem_limit_bytes=52 * MIB),
        cost_estimate=pl.CostEstimate(
            flops=2 * irreps * owned * members * 4 * cuts * depth, bytes_accessed=26 * MIB, transcendentals=0
        ),
        name="ladder",
    )(live_pairs, amplitudes, integrals)


def solution(mesh):
    in_specs = (P(None, None, ("rep", "wide"), None), P(None, "rep", "wide"), P())
    out_specs = P(None, ("rep", "wide"), None)
    return jax.shard_map(
        functools.partial(per_device, mesh.shape["rep"], mesh.shape["wide"]),
        mesh=mesh, in_specs=in_specs, out_specs=out_specs, check_vma=False,
    )
```

time: 154 us -> 162 us (1.052)
  Pallas kernels: 152 us -> 160 us
  other arithmetic: 2.11 us -> 0 us
    pallas_call x1, Pallas kernels: 152 us -> 160 us  [per_device(): pl.pallas_call(functools.partial(ladder_kernel, reps, members), out_shape...]
where the time goes in v2:
time: 162 us
  Pallas kernels  160 us (99%)
    pallas_call x1, Pallas kernels, per_device(): pl.pallas_call(functools.partial(ladder_kernel, reps, members), out_shape...  160 us

profile of v2, /device:TPU:1, one launch (start us, length us, event | category | flops | bytes accessed | tf_op | source)
XLA Modules:
  0.0 161.7 jit_solution(2787342153139740290)
XLA Ops:
  0.0 0.0 copy-start
  0.0 0.7 copy-done
  0.7 160.4 %ladder.1 = bf16[8,4,768]{2,1,0:T(4,128)(2,1)S(1)} custom-call(s32[8]{0:T(128)S(1)} %copy-done, bf16[8,32,4,2560]{3,2,1,0:T(4,128)(2,1)} %amp.1, bf16[8,192,2560]{2,1,0:T(8,128)(2,1)} %integ.1), custom_call_target="tpu_custom_call" | custom-call | flops 4026531840 | bytes 27262976 | tf_op jit(solution)/shard_map/ladder/pallas_call | solution.py:306
  161.1 0.6 copy.5
Async XLA Ops:
  0.0 0.7 copy-start

commit v3 on v2

--- a/solution.py
+++ b/solution.py
@@ -116,10 +116,6 @@
     def took(half, role, slot):
         wait_for(rows.at[half, role, slot], y_recv.at[half, role, slot - 1])
 
-    def sent(half, slot):
-        for role in range(2):
-            wait_for(rows.at[half, role, slot], y_send.at[half, role, slot - 1])
-
     def group_at(step):
         return pl.ds((plane + step) % groups * GROUP, GROUP)
 
@@ -142,13 +138,15 @@
             left = rows[1, role, 3, at].reshape(GROUP * owned, depth)
             part[1, role, at, 3] = product(left, 1, role).reshape(GROUP, owned, 2 * cuts)
 
-    def give(half, role, slots):
-        send, recv = r_send.at[half, role], r_recv.at[half, role]
-        pltpu.make_async_copy(part.at[half, role, w, slots], landed.at[half, role, w, slots], recv).start()
+    stages = (pl.ds(0, 2), pl.ds(2, 1), pl.ds(3, 1))
+
+    def give(half, stage):
+        slots, send, recv = stages[stage], r_send.at[half, stage], r_recv.at[half, stage]
+        pltpu.make_async_copy(part.at[half, :, w, slots], landed.at[half, :, w, slots], recv).start()
 
         def one(t, carry):
             remote(
-                part.at[half, role, other(t), slots], landed.at[half, role, w, slots], send, recv, r, other(t)
+                part.at[half, :, other(t), slots], landed.at[half, :, w, slots], send, recv, r, other(t)
             ).start()
             return carry
 
@@ -173,24 +171,28 @@
 
         lax.fori_loop(0, GROUP, one, 0)
 
-    def add_up(half, role, slots):
-        wait_for(landed.at[half, role, :, slots], r_recv.at[half, role])
-        summed[half, role, slots] = jnp.sum(landed[half, role, :, slots], axis=0)
+    def add_up(half, stage):
+        slots = stages[stage]
+        wait_for(landed.at[half, :, :, slots], r_recv.at[half, stage])
+        summed[half, :, slots] = jnp.sum(landed[half, :, :, slots], axis=1)
+        hand_out(half, ((0, 1), (2,), (3,))[stage])
 
     far = pl.ds(GROUP, members - GROUP)
 
     def add_up_pieces():
         wait_for(landed.at[1, :, far, 3], l_recv)
         summed[1, :, 3] = jnp.sum(landed[1, :, far, 3], axis=1)
-
-    def hand_out(half, role, slots):
-        g = irrep(role, half)
-        for slot in slots:
-            if slot == 0:
-                placed[g, role] = summed[half, role, 0]
-            else:
-                remote(summed.at[half, role, slot], placed.at[g, role], o_send.at[half, role, slot - 1],
-                       o_recv.at[half], beside[slot][role], w).start()
+        hand_out(1, (3,))
+
+    def hand_out(half, slots):
+        for role in range(2):
+            g = irrep(role, half)
+            for slot in slots:
+                if slot == 0:
+                    placed[g, role] = summed[half, role, 0]
+                else:
+                    remote(summed.at[half, role, slot], placed.at[g, role], o_send.at[half, role, slot - 1],
+                           o_recv.at[half], beside[slot][role], w).start()
 
     def finish(half):
         index = (r * members + w) * owned + lax.broadcasted_iota(jnp.int32, (owned, reps * cuts), 0)
@@ -204,8 +206,6 @@
             ladder = jnp.concatenate([found[q] for q in range(reps)], axis=1)
             out[g] = jnp.where(index < live[g], ladder, 0.0).astype(out.dtype)
 
-    every, early = pl.ds(0, 4), pl.ds(0, 3)
-
     send_columns(0)
     spread(3, 0)
     spread(2, 0)
@@ -215,51 +215,49 @@
     spread(3, 1)
     spread(2, 1)
     relay_rows(0)
-    relay_rows(1)
     send_columns(1)
     spread(0, 0)
     spread(1, 0)
+    relay_rows(1)
     spread(0, 1)
     spread(1, 1)
     forward_rows(0)
     exchange_rows(0)
-    forward_rows(1)
 
     columns_ready(0)
     for role in range(2):
         multiply(0, role, 0)
         multiply(0, role, 1)
+    give(0, 0)
+    forward_rows(1)
+    arrived(0, 1)
+    arrived(1, 1)
+    for step in (1, 2, 3, 0):
+        exchange_piece(step)
+    add_up(0, 0)
+    columns_ready(1)
+    for role in range(2):
+        multiply(1, role, 0)
+        multiply(1, role, 1)
+    give(1, 0)
     for role in range(2):
         took(0, role, 2)
         multiply(0, role, 2)
-    arrived(0, 1)
-    arrived(1, 1)
-    columns_ready(1)
-    for role in range(2):
-        multiply(1, role, 0)
-        multiply(1, role, 1)
-    sent(0, 3)
-    exchange_piece(1)
-    exchange_piece(2)
+    give(0, 1)
+    add_up(1, 0)
     for role in range(2):
         took(0, role, 3)
         multiply(0, role, 3)
-        give(0, role, every)
-    for role in range(2):
-        add_up(0, role, every)
-        hand_out(0, role, range(4))
-    sent(1, 2)
-    exchange_piece(3)
-    exchange_piece(0)
+    give(0, 2)
+    add_up(0, 1)
     for role in range(2):
         took(1, role, 2)
         multiply(1, role, 2)
-        give(1, role, early)
+    give(1, 1)
+    add_up(0, 2)
     multiply_piece(1)
     give_piece(1)
-    for role in range(2):
-        add_up(1, role, early)
-        hand_out(1, role, range(3))
+    add_up(1, 1)
     multiply_piece(2)
     give_piece(2)
     wait_for(placed.at[pl.ds(0, reps - 1)], o_recv.at[0])
@@ -269,8 +267,6 @@
     multiply_piece(0)
     give_direct()
     add_up_pieces()
-    for role in range(2):
-        hand_out(1, role, (3,))
     wait_for(direct, d_recv)
     wait_for(placed.at[pl.ds(reps, reps - 1)], o_recv.at[1])
     for role, behind in ((0, 1), (1, 0)):
@@ -278,21 +274,21 @@
         placed[g, role] = placed[g, role] + jnp.sum(direct[role], axis=0)
     finish(1)
 
+    some = pl.ds(1, members - 1)
     for half in range(halves):
         for role in range(2):
             wait_for(cols.at[half, role, theirs], b_send.at[half, role])
             for slot in range(3):
                 wait_for(summed.at[half, role, slot], o_send.at[half, role, slot])
+                if (half, slot) != (1, 2):
+                    wait_for(rows.at[half, role, slot], y_send.at[half, role, slot])
         for behind in range(reps):
-            wait_for(relay.at[half, 0, pl.ds(1, members - 1)], a_send.at[half, behind])
-        sent(half, 1)
-    sent(0, 2)
-    some = pl.ds(1, members - 1)
+            wait_for(relay.at[half, 0, some], a_send.at[half, behind])
+        for stage in range(3 - half):
+            wait_for(landed.at[half, :, some, stages[stage]], r_send.at[half, stage])
     for role in range(2):
         for step in range(groups):
             wait_for(rows.at[1, role, 0, group_at(step)], p_send.at[role, step])
-        wait_for(landed.at[0, role, some, every], r_send.at[0, role])
-        wait_for(landed.at[1, role, some, early], r_send.at[1, role])
     wait_for(landed.at[1, :, far, 3], l_send)
     wait_for(direct, d_send)
 
@@ -321,7 +317,7 @@
             dma((halves, 4)), dma((halves, 4)),
             dma((halves, 2, 3)), dma((halves, 2, 3)),
             dma((2, 4)), dma((2, 4)),
-            dma((halves, 2)), dma((halves, 2)),
+            dma((halves, 3)), dma((halves, 3)),
             dma, dma,
             dma((halves, 2, 3)), dma((halves,)),
             dma, dma,

time: 162 us -> 150 us (0.926)
  Pallas kernels: 160 us -> 149 us
    pallas_call x1, Pallas kernels: 160 us -> 149 us  [per_device(): pl.pallas_call(functools.partial(ladder_kernel, reps, members), out_shape...]
where the time goes in v3:
time: 150 us
  Pallas kernels  149 us (99%)
    pallas_call x1, Pallas kernels, per_device(): pl.pallas_call(functools.partial(ladder_kernel, reps, members), out_shape...  149 us

profile of v3, /device:TPU:1, one launch (start us, length us, event | category | flops | bytes accessed | tf_op | source)
XLA Modules:
  0.0 149.8 jit_solution(9204405528216388052)
XLA Ops:
  0.0 0.0 copy-start
  0.0 0.7 copy-done
  0.7 148.5 %ladder.1 = bf16[8,4,768]{2,1,0:T(4,128)(2,1)S(1)} custom-call(s32[8]{0:T(128)S(1)} %copy-done, bf16[8,32,4,2560]{3,2,1,0:T(4,128)(2,1)} %amp.1, bf16[8,192,2560]{2,1,0:T(8,128)(2,1)} %integ.1), custom_call_target="tpu_custom_call" | custom-call | flops 4026531840 | bytes 27262976 | tf_op jit(solution)/shard_map/ladder/pallas_call | solution.py:302
  149.2 0.6 copy.5
Async XLA Ops:
  0.0 0.7 copy-start

commit v4 on v3

--- a/solution.py
+++ b/solution.py
@@ -14,7 +14,7 @@
 
 def ladder_kernel(reps, members, live, amp, integ, out, rows, relay, cols, part, landed, summed, placed, direct,
                   b_send, b_recv, b_own, a_send, a_recv, y_send, y_recv, p_send, p_recv,
-                  r_send, r_recv, l_send, l_recv, o_send, o_recv, d_send, d_recv):
+                  r_send, r_recv, l_send, l_recv, o_send, o_recv, d_send, d_recv, counts, c_got):
     r, w = lax.axis_index("rep"), lax.axis_index("wide")
     up, down, across = (r + 1) % reps, (r + reps - 1) % reps, (r + 2) % reps
     groups = members // GROUP
@@ -41,6 +41,8 @@
     def neighbour(t):
         return plane * GROUP + (seat + t) % GROUP
 
+    fetch = pltpu.make_async_copy(live, counts, c_got)
+    fetch.start()
     barrier = pltpu.get_barrier_semaphore()
 
     def greet(rep, member):
@@ -61,6 +63,10 @@
     pl.semaphore_wait(barrier, members + 2 * GROUP)
 
     mine, theirs = pl.ds(0, cuts), pl.ds(cuts, cuts)
+    near, far = pl.ds(0, GROUP), pl.ds(GROUP, members - GROUP)
+    far_steps = ((1, 2), (3,))
+    far_pieces = (pl.ds(GROUP, 2 * GROUP), pl.ds(3 * GROUP, GROUP))
+    stretches = (pl.ds(0, depth // 2), pl.ds(depth // 2, depth // 2))
 
     def send_columns(half):
         remote(integ.at[irrep(3, half)], cols.at[half, 0, theirs], b_send.at[half, 0], b_recv.at[half, 0], up, w).start()
@@ -119,10 +125,16 @@
     def group_at(step):
         return pl.ds((plane + step) % groups * GROUP, GROUP)
 
-    def exchange_piece(step):
+    def exchange_far(piece):
         for role, rep in ((0, up), (1, down)):
-            remote(rows.at[1, role, 0, group_at(step)], rows.at[1, 1 - role, 3, group_at(step)],
-                   p_send.at[role, step], p_recv.at[1 - role, step], rep, w).start()
+            for step in far_steps[piece]:
+                remote(rows.at[1, role, 0, group_at(step)], rows.at[1, 1 - role, 3, pl.ds(step * GROUP, GROUP)],
+                       p_send.at[role, piece], p_recv.at[1 - role, piece], rep, w).start()
+
+    def exchange_near(stretch):
+        for role, rep in ((0, up), (1, down)):
+            remote(rows.at[1, role, 0, group_at(0), :, stretches[stretch]], rows.at[1, 1 - role, 3, near, :, stretches[stretch]],
+                   p_send.at[role, 2 + stretch], p_recv.at[1 - role, 2 + stretch], rep, w).start()
 
     def product(left, half, role):
         return lax.dot_general(left, cols[half, role], (((1,), (1,)), ((), ())), preferred_element_type=jnp.float32)
@@ -131,12 +143,21 @@
         left = rows[half, role, slot].reshape(members * owned, depth)
         part[half, role, :, slot] = product(left, half, role).reshape(members, owned, 2 * cuts)
 
-    def multiply_piece(step):
-        for role in range(2):
-            at = group_at(step)
-            wait_for(rows.at[1, role, 3, at], p_recv.at[role, step])
-            left = rows[1, role, 3, at].reshape(GROUP * owned, depth)
-            part[1, role, at, 3] = product(left, 1, role).reshape(GROUP, owned, 2 * cuts)
+    def multiply_far(piece):
+        at = far_pieces[piece]
+        for role in range(2):
+            wait_for(rows.at[1, role, 3, at], p_recv.at[role, piece])
+            left = rows[1, role, 3, at].reshape(at.size * owned, depth)
+            part[1, role, at, 3] = product(left, 1, role).reshape(at.size, owned, 2 * cuts)
+
+    def multiply_near(role, stretch):
+        inner = stretches[stretch]
+        wait_for(rows.at[1, role, 3, near, :, inner], p_recv.at[role, 2 + stretch])
+        left = rows[1, role, 3, near, :, inner].reshape(GROUP * owned, depth // 2)
+        some = lax.dot_general(
+            left, cols[1, role, :, inner], (((1,), (1,)), ((), ())), preferred_element_type=jnp.float32
+        ).reshape(GROUP, owned, 2 * cuts)
+        part[1, role, near, 3] = some if stretch == 0 else part[1, role, near, 3] + some
 
     stages = (pl.ds(0, 2), pl.ds(2, 1), pl.ds(3, 1))
 
@@ -152,21 +173,21 @@
 
         lax.fori_loop(1, members, one, 0)
 
-    def give_piece(step):
-        base = (plane + step) % groups * GROUP
-
+    def give_far(piece):
         def one(t, carry):
-            member = base + (seat + t) % GROUP
-            remote(part.at[1, :, member, 3], landed.at[1, :, step * GROUP + seat, 3], l_send, l_recv, r, member).start()
+            step, place = t // GROUP, (seat + t) % GROUP
+            member = (plane + step) % groups * GROUP + place
+            remote(part.at[1, :, step * GROUP + place, 3], landed.at[1, :, step * GROUP + seat, 3], l_send, l_recv,
+                   r, member).start()
             return carry
 
-        lax.fori_loop(0, GROUP, one, 0)
-
-    def give_direct():
+        at = far_pieces[piece]
+        lax.fori_loop(at.start, at.start + at.size, one, 0)
+
+    def give_near(role):
         def one(t, carry):
-            for role in range(2):
-                remote(part.at[1, role, neighbour(t), 3], direct.at[role, seat], d_send, d_recv,
-                       beside[3][role], neighbour(t)).start()
+            remote(part.at[1, role, (seat + t) % GROUP, 3], direct.at[role, seat], d_send.at[role], d_recv.at[role],
+                   beside[3][role], neighbour(t)).start()
             return carry
 
         lax.fori_loop(0, GROUP, one, 0)
@@ -177,9 +198,7 @@
         summed[half, :, slots] = jnp.sum(landed[half, :, :, slots], axis=1)
         hand_out(half, ((0, 1), (2,), (3,))[stage])
 
-    far = pl.ds(GROUP, members - GROUP)
-
-    def add_up_pieces():
+    def add_up_far():
         wait_for(landed.at[1, :, far, 3], l_recv)
         summed[1, :, 3] = jnp.sum(landed[1, :, far, 3], axis=1)
         hand_out(1, (3,))
@@ -204,7 +223,7 @@
                 found[here] = placed[g, role, :, :cuts]
                 found[(here + beyond) % reps] = placed[g, role, :, cuts:]
             ladder = jnp.concatenate([found[q] for q in range(reps)], axis=1)
-            out[g] = jnp.where(index < live[g], ladder, 0.0).astype(out.dtype)
+            out[g] = jnp.where(index < counts[g], ladder, 0.0).astype(out.dtype)
 
     send_columns(0)
     spread(3, 0)
@@ -232,8 +251,6 @@
     forward_rows(1)
     arrived(0, 1)
     arrived(1, 1)
-    for step in (1, 2, 3, 0):
-        exchange_piece(step)
     add_up(0, 0)
     columns_ready(1)
     for role in range(2):
@@ -250,47 +267,61 @@
         multiply(0, role, 3)
     give(0, 2)
     add_up(0, 1)
+    exchange_far(0)
     for role in range(2):
         took(1, role, 2)
         multiply(1, role, 2)
     give(1, 1)
     add_up(0, 2)
-    multiply_piece(1)
-    give_piece(1)
+    exchange_far(1)
+    exchange_near(0)
+    exchange_near(1)
+    some = pl.ds(1, members - 1)
+    for half in range(halves):
+        for role in range(2):
+            wait_for(cols.at[half, role, theirs], b_send.at[half, role])
+            wait_for(rows.at[half, role, 0], y_send.at[half, role, 0])
+        for behind in range(reps):
+            wait_for(relay.at[half, 0, some], a_send.at[half, behind])
+        wait_for(landed.at[half, :, some, stages[0]], r_send.at[half, 0])
+    for stage in (1, 2):
+        wait_for(landed.at[0, :, some, stages[stage]], r_send.at[0, stage])
+        for role in range(2):
+            wait_for(rows.at[0, role, 0], y_send.at[0, role, stage])
+    multiply_far(0)
+    give_far(0)
     add_up(1, 1)
-    multiply_piece(2)
-    give_piece(2)
+    fetch.wait()
     wait_for(placed.at[pl.ds(0, reps - 1)], o_recv.at[0])
     finish(0)
-    multiply_piece(3)
-    give_piece(3)
-    multiply_piece(0)
-    give_direct()
-    add_up_pieces()
-    wait_for(direct, d_recv)
+    multiply_far(1)
+    give_far(1)
+    for role in range(2):
+        multiply_near(role, 0)
+    for role in range(2):
+        multiply_near(role, 1)
+        give_near(role)
+    add_up_far()
+    for role in range(2):
+        wait_for(rows.at[1, role, 0], y_send.at[1, role, 1])
+        for index in range(2):
+            wait_for(rows.at[1, role, 0, far_pieces[index]], p_send.at[role, index])
+            wait_for(rows.at[1, role, 0, near, :, stretches[index]], p_send.at[role, 2 + index])
+        for slot in range(3):
+            wait_for(summed.at[0, role, slot], o_send.at[0, role, slot])
+        for slot in range(2):
+            wait_for(summed.at[1, role, slot], o_send.at[1, role, slot])
+    wait_for(landed.at[1, :, some, stages[1]], r_send.at[1, 1])
+    wait_for(landed.at[1, :, far, 3], l_send)
+    for role in range(2):
+        wait_for(direct.at[role], d_send.at[role])
+        wait_for(direct.at[role], d_recv.at[role])
+        wait_for(summed.at[1, role, 2], o_send.at[1, role, 2])
     wait_for(placed.at[pl.ds(reps, reps - 1)], o_recv.at[1])
     for role, behind in ((0, 1), (1, 0)):
         g = irrep(behind, 1)
         placed[g, role] = placed[g, role] + jnp.sum(direct[role], axis=0)
     finish(1)
-
-    some = pl.ds(1, members - 1)
-    for half in range(halves):
-        for role in range(2):
-            wait_for(cols.at[half, role, theirs], b_send.at[half, role])
-            for slot in range(3):
-                wait_for(summed.at[half, role, slot], o_send.at[half, role, slot])
-                if (half, slot) != (1, 2):
-                    wait_for(rows.at[half, role, slot], y_send.at[half, role, slot])
-        for behind in range(reps):
-            wait_for(relay.at[half, 0, some], a_send.at[half, behind])
-        for stage in range(3 - half):
-            wait_for(landed.at[half, :, some, stages[stage]], r_send.at[half, stage])
-    for role in range(2):
-        for step in range(groups):
-            wait_for(rows.at[1, role, 0, group_at(step)], p_send.at[role, step])
-    wait_for(landed.at[1, :, far, 3], l_send)
-    wait_for(direct, d_send)
 
 
 def per_device(reps, members, amplitudes, integrals, live_pairs):
@@ -302,7 +333,7 @@
     return pl.pallas_call(
         functools.partial(ladder_kernel, reps, members),
         out_shape=jax.ShapeDtypeStruct((irreps, owned, reps * cuts), bf16),
-        in_specs=[pl.BlockSpec(memory_space=pltpu.SMEM)] + [pl.BlockSpec(memory_space=pl.ANY)] * 2,
+        in_specs=[pl.BlockSpec(memory_space=pl.ANY)] * 3,
         out_specs=pl.BlockSpec(memory_space=pltpu.VMEM),
         scratch_shapes=[
             pltpu.VMEM((halves, 2, 4, members, owned, depth), bf16),
@@ -320,7 +351,8 @@
             dma((halves, 3)), dma((halves, 3)),
             dma, dma,
             dma((halves, 2, 3)), dma((halves,)),
-            dma, dma,
+            dma((2,)), dma((2,)),
+            pltpu.SMEM((irreps,), jnp.int32), dma,
         ],
         compiler_params=pltpu.CompilerParams(collective_id=0, has_side_effects=True, vmem_limit_bytes=52 * MIB),
         cost_estimate=pl.CostEstimate(

time: 150 us -> 145 us (0.967)
  Pallas kernels: 149 us -> 144 us
    pallas_call x1, Pallas kernels: 149 us -> 144 us  [per_device(): pl.pallas_call(functools.partial(ladder_kernel, reps, members), out_shape...]
where the time goes in v4:
time: 145 us
  Pallas kernels  144 us (99%)
    pallas_call x1, Pallas kernels, per_device(): pl.pallas_call(functools.partial(ladder_kernel, reps, members), out_shape...  144 us

profile of v4, /device:TPU:1, one launch (start us, length us, event | category | flops | bytes accessed | tf_op | source)
XLA Modules:
  0.0 144.8 jit_solution(7003577350046571364)
XLA Ops:
  0.0 0.0 copy-start
  0.0 0.7 copy-done
  0.7 143.5 %ladder.1 = bf16[8,4,768]{2,1,0:T(4,128)(2,1)S(1)} custom-call(s32[8]{0:T(128)S(1)} %copy-done, bf16[8,32,4,2560]{3,2,1,0:T(4,128)(2,1)} %amp.1, bf16[8,192,2560]{2,1,0:T(8,128)(2,1)} %integ.1), custom_call_target="tpu_custom_call" | custom-call | flops 4026531840 | bytes 27262976 | tf_op jit(solution)/shard_map/ladder/pallas_call | solution.py:333
  144.2 0.6 copy.5
Async XLA Ops:
  0.0 0.7 copy-start

commit v5 on v4

--- a/solution.py
+++ b/solution.py
@@ -12,9 +12,9 @@
 GROUP = 8
 
 
-def ladder_kernel(reps, members, live, amp, integ, out, rows, relay, cols, part, landed, summed, placed, direct,
+def ladder_kernel(reps, members, amp, integ, out, rows, relay, cols, part, landed, summed, placed, direct,
                   b_send, b_recv, b_own, a_send, a_recv, y_send, y_recv, p_send, p_recv,
-                  r_send, r_recv, l_send, l_recv, o_send, o_recv, d_send, d_recv, counts, c_got):
+                  r_send, r_recv, l_send, l_recv, o_send, o_recv, d_send, d_recv):
     r, w = lax.axis_index("rep"), lax.axis_index("wide")
     up, down, across = (r + 1) % reps, (r + reps - 1) % reps, (r + 2) % reps
     groups = members // GROUP
@@ -38,11 +38,6 @@
     def other(t):
         return (w + t) % members
 
-    def neighbour(t):
-        return plane * GROUP + (seat + t) % GROUP
-
-    fetch = pltpu.make_async_copy(live, counts, c_got)
-    fetch.start()
     barrier = pltpu.get_barrier_semaphore()
 
     def greet(rep, member):
@@ -52,18 +47,13 @@
         greet(r, other(t))
         return carry
 
-    def greet_group(t, carry):
-        greet(up, neighbour(t))
-        greet(down, neighbour(t))
-        return carry
-
-    greet(across, w)
-    lax.fori_loop(0, GROUP, greet_group, 0)
+    greet(up, w)
+    greet(down, w)
     lax.fori_loop(1, members, greet_rep, 0)
-    pl.semaphore_wait(barrier, members + 2 * GROUP)
+    pl.semaphore_wait(barrier, members + 1)
 
     mine, theirs = pl.ds(0, cuts), pl.ds(cuts, cuts)
-    near, far = pl.ds(0, GROUP), pl.ds(GROUP, members - GROUP)
+    near = pl.ds(0, GROUP)
     far_steps = ((1, 2), (3,))
     far_pieces = (pl.ds(GROUP, 2 * GROUP), pl.ds(3 * GROUP, GROUP))
     stretches = (pl.ds(0, depth // 2), pl.ds(depth // 2, depth // 2))
@@ -173,7 +163,7 @@
 
         lax.fori_loop(1, members, one, 0)
 
-    def give_far(piece):
+    def give_far():
         def one(t, carry):
             step, place = t // GROUP, (seat + t) % GROUP
             member = (plane + step) % groups * GROUP + place
@@ -181,13 +171,14 @@
                    r, member).start()
             return carry
 
-        at = far_pieces[piece]
+        at = far_pieces[0]
         lax.fori_loop(at.start, at.start + at.size, one, 0)
 
-    def give_near(role):
+    def give_direct(role, step, kept):
         def one(t, carry):
-            remote(part.at[1, role, (seat + t) % GROUP, 3], direct.at[role, seat], d_send.at[role], d_recv.at[role],
-                   beside[3][role], neighbour(t)).start()
+            place = (seat + t) % GROUP
+            remote(part.at[1, role, step * GROUP + place, 3], direct.at[role, kept, seat], d_send.at[role],
+                   d_recv.at[role], beside[3][role], (plane + step) % groups * GROUP + place).start()
             return carry
 
         lax.fori_loop(0, GROUP, one, 0)
@@ -199,8 +190,8 @@
         hand_out(half, ((0, 1), (2,), (3,))[stage])
 
     def add_up_far():
-        wait_for(landed.at[1, :, far, 3], l_recv)
-        summed[1, :, 3] = jnp.sum(landed[1, :, far, 3], axis=1)
+        wait_for(landed.at[1, :, far_pieces[0], 3], l_recv)
+        summed[1, :, 3] = jnp.sum(landed[1, :, far_pieces[0], 3], axis=1)
         hand_out(1, (3,))
 
     def hand_out(half, slots):
@@ -214,7 +205,6 @@
                            o_recv.at[half], beside[slot][role], w).start()
 
     def finish(half):
-        index = (r * members + w) * owned + lax.broadcasted_iota(jnp.int32, (owned, reps * cuts), 0)
         for p in range(reps):
             g = reps * half + p
             found = {}
@@ -222,8 +212,7 @@
                 here = (p + role) % reps
                 found[here] = placed[g, role, :, :cuts]
                 found[(here + beyond) % reps] = placed[g, role, :, cuts:]
-            ladder = jnp.concatenate([found[q] for q in range(reps)], axis=1)
-            out[g] = jnp.where(index < counts[g], ladder, 0.0).astype(out.dtype)
+            out[g] = jnp.concatenate([found[q] for q in range(reps)], axis=1).astype(out.dtype)
 
     send_columns(0)
     spread(3, 0)
@@ -289,18 +278,18 @@
         for role in range(2):
             wait_for(rows.at[0, role, 0], y_send.at[0, role, stage])
     multiply_far(0)
-    give_far(0)
+    give_far()
     add_up(1, 1)
-    fetch.wait()
     wait_for(placed.at[pl.ds(0, reps - 1)], o_recv.at[0])
     finish(0)
     multiply_far(1)
-    give_far(1)
+    for role in range(2):
+        give_direct(role, 3, 1)
     for role in range(2):
         multiply_near(role, 0)
     for role in range(2):
         multiply_near(role, 1)
-        give_near(role)
+        give_direct(role, 0, 0)
     add_up_far()
     for role in range(2):
         wait_for(rows.at[1, role, 0], y_send.at[1, role, 1])
@@ -312,7 +301,7 @@
         for slot in range(2):
             wait_for(summed.at[1, role, slot], o_send.at[1, role, slot])
     wait_for(landed.at[1, :, some, stages[1]], r_send.at[1, 1])
-    wait_for(landed.at[1, :, far, 3], l_send)
+    wait_for(landed.at[1, :, far_pieces[0], 3], l_send)
     for role in range(2):
         wait_for(direct.at[role], d_send.at[role])
         wait_for(direct.at[role], d_recv.at[role])
@@ -320,7 +309,7 @@
     wait_for(placed.at[pl.ds(reps, reps - 1)], o_recv.at[1])
     for role, behind in ((0, 1), (1, 0)):
         g = irrep(behind, 1)
-        placed[g, role] = placed[g, role] + jnp.sum(direct[role], axis=0)
+        placed[g, role] = placed[g, role] + jnp.sum(direct[role], axis=(0, 1))
     finish(1)
 
 
@@ -330,10 +319,10 @@
     halves = irreps // reps
     dma = pltpu.SemaphoreType.DMA
     f32, bf16 = jnp.float32, jnp.bfloat16
-    return pl.pallas_call(
+    sums = pl.pallas_call(
         functools.partial(ladder_kernel, reps, members),
         out_shape=jax.ShapeDtypeStruct((irreps, owned, reps * cuts), bf16),
-        in_specs=[pl.BlockSpec(memory_space=pl.ANY)] * 3,
+        in_specs=[pl.BlockSpec(memory_space=pl.ANY)] * 2,
         out_specs=pl.BlockSpec(memory_space=pltpu.VMEM),
         scratch_shapes=[
             pltpu.VMEM((halves, 2, 4, members, owned, depth), bf16),
@@ -343,7 +332,7 @@
             pltpu.VMEM((halves, 2, members, 4, owned, 2 * cuts), f32),
             pltpu.VMEM((halves, 2, 4, owned, 2 * cuts), f32),
             pltpu.VMEM((irreps, 2, owned, 2 * cuts), f32),
-            pltpu.VMEM((2, GROUP, owned, 2 * cuts), f32),
+            pltpu.VMEM((2, 2, GROUP, owned, 2 * cuts), f32),
             dma((halves, 2)), dma((halves, 2)), dma((halves, 2)),
             dma((halves, 4)), dma((halves, 4)),
             dma((halves, 2, 3)), dma((halves, 2, 3)),
@@ -352,14 +341,17 @@
             dma, dma,
             dma((halves, 2, 3)), dma((halves,)),
             dma((2,)), dma((2,)),
-            pltpu.SMEM((irreps,), jnp.int32), dma,
         ],
         compiler_params=pltpu.CompilerParams(collective_id=0, has_side_effects=True, vmem_limit_bytes=52 * MIB),
         cost_estimate=pl.CostEstimate(
             flops=2 * irreps * owned * members * 4 * cuts * depth, bytes_accessed=26 * MIB, transcendentals=0
         ),
         name="ladder",
-    )(live_pairs, amplitudes, integrals)
+    )(amplitudes, integrals)
+    sums, live_pairs = lax.optimization_barrier((sums, live_pairs))
+    first = (lax.axis_index("rep") * members + lax.axis_index("wide")) * owned
+    index = first + lax.broadcasted_iota(jnp.int32, sums.shape, 1)
+    return jnp.where(index < live_pairs[:, None, None], sums, jnp.zeros_like(sums))
 
 
 def solution(mesh):

time: 145 us -> 144 us (level)
  no operation moved by 1% of the time
where the time goes in v5:
time: 144 us
  Pallas kernels  144 us (100%)
    pallas_call x1, Pallas kernels, per_device(): pl.pallas_call(functools.partial(ladder_kernel, reps, members), out_shape...  144 us

profile of v5, /device:TPU:1, one launch (start us, length us, event | category | flops | bytes accessed | tf_op | source)
XLA Modules:
  0.0 144.3 jit_solution(16372133521673858286)
XLA Ops:
  0.0 0.0 copy-start
  0.0 143.6 %ladder.1 = bf16[8,4,768]{2,1,0:T(4,128)(2,1)S(1)} custom-call(bf16[8,32,4,2560]{3,2,1,0:T(4,128)(2,1)} %amp.1, bf16[8,192,2560]{2,1,0:T(8,128)(2,1)} %integ.1), custom_call_target="tpu_custom_call" | custom-call | flops 4026531840 | bytes 27262976 | tf_op jit(solution)/shard_map/ladder/pallas_call | solution.py:322
  143.6 0.0 copy-done
  143.6 0.7 compare_select_fusion
  (1 shorter events, 0.0 us)
Async XLA Ops:
  0.0 143.6 %copy-start = (s32[8]{0:T(128)S(1)}, s32[8]{0:T(128)}, u32[]{:S(2)}) copy-start(s32[8]{0:T(128)} %param.5) | copy-start | bytes 100

commit v6 on v5

--- a/solution.py
+++ b/solution.py
@@ -14,7 +14,7 @@
 
 def ladder_kernel(reps, members, amp, integ, out, rows, relay, cols, part, landed, summed, placed, direct,
                   b_send, b_recv, b_own, a_send, a_recv, y_send, y_recv, p_send, p_recv,
-                  r_send, r_recv, l_send, l_recv, o_send, o_recv, d_send, d_recv):
+                  r_send, r_recv, l_send, l_recv, o_send, o_recv, d_send, d_recv, ready):
     r, w = lax.axis_index("rep"), lax.axis_index("wide")
     up, down, across = (r + 1) % reps, (r + reps - 1) % reps, (r + 2) % reps
     groups = members // GROUP
@@ -43,14 +43,44 @@
     def greet(rep, member):
         pl.semaphore_signal(barrier, inc=1, device_id=(rep, member), device_id_type=MESH)
 
-    def greet_rep(t, carry):
-        greet(r, other(t))
-        return carry
-
     greet(up, w)
     greet(down, w)
-    lax.fori_loop(1, members, greet_rep, 0)
-    pl.semaphore_wait(barrier, members + 1)
+    for t in range(1, GROUP):
+        greet(r, plane * GROUP + (seat + t) % GROUP)
+
+    def each_after(act):
+        for step in range(1, groups):
+            @pl.when(plane + step < groups)
+            def _():
+                act(w + step * GROUP)
+
+    def each_before(act):
+        for step in range(1, groups):
+            @pl.when(plane >= step)
+            def _():
+                act(w - step * GROUP)
+
+    def tell(sem):
+        def one(member):
+            pl.semaphore_signal(sem, inc=1, device_id=(r, member), device_id_type=MESH)
+
+        return one
+
+    each_after(functools.partial(greet, r))
+    pl.semaphore_wait(barrier, GROUP + 1 + plane)
+
+    def meet_plane():
+        each_before(tell(ready.at[0]))
+
+        @pl.when(plane < groups - 1)
+        def _():
+            pl.semaphore_wait(ready.at[0], groups - 1 - plane)
+
+        each_after(tell(ready.at[1]))
+
+        @pl.when(plane > 0)
+        def _():
+            pl.semaphore_wait(ready.at[1], plane)
 
     mine, theirs = pl.ds(0, cuts), pl.ds(cuts, cuts)
     near = pl.ds(0, GROUP)
@@ -215,6 +245,8 @@
             out[g] = jnp.concatenate([found[q] for q in range(reps)], axis=1).astype(out.dtype)
 
     send_columns(0)
+    send_columns(1)
+    meet_plane()
     spread(3, 0)
     spread(2, 0)
     for half in range(halves):
@@ -223,7 +255,6 @@
     spread(3, 1)
     spread(2, 1)
     relay_rows(0)
-    send_columns(1)
     spread(0, 0)
     spread(1, 0)
     relay_rows(1)
@@ -279,17 +310,17 @@
             wait_for(rows.at[0, role, 0], y_send.at[0, role, stage])
     multiply_far(0)
     give_far()
+    multiply_far(1)
+    for role in range(2):
+        give_direct(role, 3, 1)
+    for role in range(2):
+        multiply_near(role, 0)
+    for role in range(2):
+        multiply_near(role, 1)
+        give_direct(role, 0, 0)
     add_up(1, 1)
     wait_for(placed.at[pl.ds(0, reps - 1)], o_recv.at[0])
     finish(0)
-    multiply_far(1)
-    for role in range(2):
-        give_direct(role, 3, 1)
-    for role in range(2):
-        multiply_near(role, 0)
-    for role in range(2):
-        multiply_near(role, 1)
-        give_direct(role, 0, 0)
     add_up_far()
     for role in range(2):
         wait_for(rows.at[1, role, 0], y_send.at[1, role, 1])
@@ -340,7 +371,7 @@
             dma((halves, 3)), dma((halves, 3)),
             dma, dma,
             dma((halves, 2, 3)), dma((halves,)),
-            dma((2,)), dma((2,)),
+            dma((2,)), dma((2,)), pltpu.SemaphoreType.REGULAR((2,)),
         ],
         compiler_params=pltpu.CompilerParams(collective_id=0, has_side_effects=True, vmem_limit_bytes=52 * MIB),
         cost_estimate=pl.CostEstimate(

time: 144 us -> 143 us (level)
  Pallas kernels: 144 us -> 142 us
    pallas_call x1, Pallas kernels: 144 us -> 142 us  [per_device(): pl.pallas_call(functools.partial(ladder_kernel, reps, members), out_shape...]
where the time goes in v6:
time: 143 us
  Pallas kernels  142 us (99%)
    pallas_call x1, Pallas kernels, per_device(): pl.pallas_call(functools.partial(ladder_kernel, reps, members), out_shape...  142 us

profile of v6, /device:TPU:1, one launch (start us, length us, event | category | flops | bytes accessed | tf_op | source)
XLA Modules:
  0.0 142.6 jit_solution(7848544446210117461)
XLA Ops:
  0.0 0.0 copy-start
  0.0 141.9 %ladder.1 = bf16[8,4,768]{2,1,0:T(4,128)(2,1)S(1)} custom-call(bf16[8,32,4,2560]{3,2,1,0:T(4,128)(2,1)} %amp.1, bf16[8,192,2560]{2,1,0:T(8,128)(2,1)} %integ.1), custom_call_target="tpu_custom_call" | custom-call | flops 4026531840 | bytes 27262976 | tf_op jit(solution)/shard_map/ladder/pallas_call | solution.py:353
  141.9 0.0 copy-done
  141.9 0.7 compare_select_fusion
  (1 shorter events, 0.0 us)
Async XLA Ops:
  0.0 141.9 %copy-start = (s32[8]{0:T(128)S(1)}, s32[8]{0:T(128)}, u32[]{:S(2)}) copy-start(s32[8]{0:T(128)} %param.5) | copy-start | bytes 100

commit v7 on v6

--- a/solution.py
+++ b/solution.py
@@ -84,8 +84,8 @@
 
     mine, theirs = pl.ds(0, cuts), pl.ds(cuts, cuts)
     near = pl.ds(0, GROUP)
-    far_steps = ((1, 2), (3,))
-    far_pieces = (pl.ds(GROUP, 2 * GROUP), pl.ds(3 * GROUP, GROUP))
+    far_planes = (2, 1, 3)
+    far_pieces = tuple(pl.ds((k + 1) * GROUP, GROUP) for k in range(3))
     stretches = (pl.ds(0, depth // 2), pl.ds(depth // 2, depth // 2))
 
     def send_columns(half):
@@ -147,14 +147,13 @@
 
     def exchange_far(piece):
         for role, rep in ((0, up), (1, down)):
-            for step in far_steps[piece]:
-                remote(rows.at[1, role, 0, group_at(step)], rows.at[1, 1 - role, 3, pl.ds(step * GROUP, GROUP)],
-                       p_send.at[role, piece], p_recv.at[1 - role, piece], rep, w).start()
+            remote(rows.at[1, role, 0, group_at(far_planes[piece])], rows.at[1, 1 - role, 3, far_pieces[piece]],
+                   p_send.at[role, piece], p_recv.at[1 - role, piece], rep, w).start()
 
     def exchange_near(stretch):
         for role, rep in ((0, up), (1, down)):
             remote(rows.at[1, role, 0, group_at(0), :, stretches[stretch]], rows.at[1, 1 - role, 3, near, :, stretches[stretch]],
-                   p_send.at[role, 2 + stretch], p_recv.at[1 - role, 2 + stretch], rep, w).start()
+                   p_send.at[role, 3 + stretch], p_recv.at[1 - role, 3 + stretch], rep, w).start()
 
     def product(left, half, role):
         return lax.dot_general(left, cols[half, role], (((1,), (1,)), ((), ())), preferred_element_type=jnp.float32)
@@ -172,7 +171,7 @@
 
     def multiply_near(role, stretch):
         inner = stretches[stretch]
-        wait_for(rows.at[1, role, 3, near, :, inner], p_recv.at[role, 2 + stretch])
+        wait_for(rows.at[1, role, 3, near, :, inner], p_recv.at[role, 3 + stretch])
         left = rows[1, role, 3, near, :, inner].reshape(GROUP * owned, depth // 2)
         some = lax.dot_general(
             left, cols[1, role, :, inner], (((1,), (1,)), ((), ())), preferred_element_type=jnp.float32
@@ -193,22 +192,24 @@
 
         lax.fori_loop(1, members, one, 0)
 
-    def give_far():
+    def give_far(piece):
+        place, base = far_pieces[piece].start, (plane + far_planes[piece]) % groups * GROUP
+
         def one(t, carry):
-            step, place = t // GROUP, (seat + t) % GROUP
-            member = (plane + step) % groups * GROUP + place
-            remote(part.at[1, :, step * GROUP + place, 3], landed.at[1, :, step * GROUP + seat, 3], l_send, l_recv,
-                   r, member).start()
+            there = (seat + t) % GROUP
+            remote(part.at[1, :, place + there, 3], landed.at[1, :, place + seat, 3], l_send, l_recv,
+                   r, base + there).start()
             return carry
 
-        at = far_pieces[0]
-        lax.fori_loop(at.start, at.start + at.size, one, 0)
-
-    def give_direct(role, step, kept):
+        lax.fori_loop(0, GROUP, one, 0)
+
+    def give_direct(role, place, step, kept):
+        base = (plane + step) % groups * GROUP
+
         def one(t, carry):
-            place = (seat + t) % GROUP
-            remote(part.at[1, role, step * GROUP + place, 3], direct.at[role, kept, seat], d_send.at[role],
-                   d_recv.at[role], beside[3][role], (plane + step) % groups * GROUP + place).start()
+            there = (seat + t) % GROUP
+            remote(part.at[1, role, place * GROUP + there, 3], direct.at[role, kept, seat], d_send.at[role],
+                   d_recv.at[role], beside[3][role], base + there).start()
             return carry
 
         lax.fori_loop(0, GROUP, one, 0)
@@ -220,8 +221,8 @@
         hand_out(half, ((0, 1), (2,), (3,))[stage])
 
     def add_up_far():
-        wait_for(landed.at[1, :, far_pieces[0], 3], l_recv)
-        summed[1, :, 3] = jnp.sum(landed[1, :, far_pieces[0], 3], axis=1)
+        wait_for(landed.at[1, :, pl.ds(GROUP, 2 * GROUP), 3], l_recv)
+        summed[1, :, 3] = jnp.sum(landed[1, :, pl.ds(GROUP, 2 * GROUP), 3], axis=1)
         hand_out(1, (3,))
 
     def hand_out(half, slots):
@@ -288,12 +289,13 @@
     give(0, 2)
     add_up(0, 1)
     exchange_far(0)
+    exchange_far(1)
     for role in range(2):
         took(1, role, 2)
         multiply(1, role, 2)
     give(1, 1)
     add_up(0, 2)
-    exchange_far(1)
+    exchange_far(2)
     exchange_near(0)
     exchange_near(1)
     some = pl.ds(1, members - 1)
@@ -308,31 +310,33 @@
         wait_for(landed.at[0, :, some, stages[stage]], r_send.at[0, stage])
         for role in range(2):
             wait_for(rows.at[0, role, 0], y_send.at[0, role, stage])
-    multiply_far(0)
-    give_far()
-    multiply_far(1)
-    for role in range(2):
-        give_direct(role, 3, 1)
+    for piece in range(2):
+        multiply_far(piece)
+        give_far(piece)
+    multiply_far(2)
+    for role in range(2):
+        give_direct(role, 3, 3, 1)
     for role in range(2):
         multiply_near(role, 0)
     for role in range(2):
         multiply_near(role, 1)
-        give_direct(role, 0, 0)
+        give_direct(role, 0, 0, 0)
     add_up(1, 1)
     wait_for(placed.at[pl.ds(0, reps - 1)], o_recv.at[0])
     finish(0)
     add_up_far()
     for role in range(2):
         wait_for(rows.at[1, role, 0], y_send.at[1, role, 1])
+        for index in range(3):
+            wait_for(rows.at[1, role, 0, far_pieces[index]], p_send.at[role, index])
         for index in range(2):
-            wait_for(rows.at[1, role, 0, far_pieces[index]], p_send.at[role, index])
-            wait_for(rows.at[1, role, 0, near, :, stretches[index]], p_send.at[role, 2 + index])
+            wait_for(rows.at[1, role, 0, near, :, stretches[index]], p_send.at[role, 3 + index])
         for slot in range(3):
             wait_for(summed.at[0, role, slot], o_send.at[0, role, slot])
         for slot in range(2):
             wait_for(summed.at[1, role, slot], o_send.at[1, role, slot])
     wait_for(landed.at[1, :, some, stages[1]], r_send.at[1, 1])
-    wait_for(landed.at[1, :, far_pieces[0], 3], l_send)
+    wait_for(landed.at[1, :, pl.ds(GROUP, 2 * GROUP), 3], l_send)
     for role in range(2):
         wait_for(direct.at[role], d_send.at[role])
         wait_for(direct.at[role], d_recv.at[role])
@@ -367,7 +371,7 @@
             dma((halves, 2)), dma((halves, 2)), dma((halves, 2)),
             dma((halves, 4)), dma((halves, 4)),
             dma((halves, 2, 3)), dma((halves, 2, 3)),
-            dma((2, 4)), dma((2, 4)),
+            dma((2, 5)), dma((2, 5)),
             dma((halves, 3)), dma((halves, 3)),
             dma, dma,
             dma((halves, 2, 3)), dma((halves,)),

time: 143 us -> 142 us (level)
  no operation moved by 1% of the time
where the time goes in v7:
time: 142 us
  Pallas kernels  141 us (99%)
    pallas_call x1, Pallas kernels, per_device(): pl.pallas_call(functools.partial(ladder_kernel, reps, members), out_shape...  141 us

profile of v7, /device:TPU:1, one launch (start us, length us, event | category | flops | bytes accessed | tf_op | source)
XLA Modules:
  0.0 142.2 jit_solution(3551301358451042132)
XLA Ops:
  0.0 0.0 copy-start
  0.0 141.4 %ladder.1 = bf16[8,4,768]{2,1,0:T(4,128)(2,1)S(1)} custom-call(bf16[8,32,4,2560]{3,2,1,0:T(4,128)(2,1)} %amp.1, bf16[8,192,2560]{2,1,0:T(8,128)(2,1)} %integ.1), custom_call_target="tpu_custom_call" | custom-call | flops 4026531840 | bytes 27262976 | tf_op jit(solution)/shard_map/ladder/pallas_call | solution.py:357
  141.4 0.0 copy-done
  141.4 0.7 compare_select_fusion
  (1 shorter events, 0.0 us)
Async XLA Ops:
  0.0 141.4 %copy-start = (s32[8]{0:T(128)S(1)}, s32[8]{0:T(128)}, u32[]{:S(2)}) copy-start(s32[8]{0:T(128)} %param.5) | copy-start | bytes 100

commit v8 on v7

--- a/solution.py
+++ b/solution.py
@@ -12,9 +12,9 @@
 GROUP = 8
 
 
-def ladder_kernel(reps, members, amp, integ, out, rows, relay, cols, part, landed, summed, placed, direct,
+def ladder_kernel(reps, members, amp, integ, out, rows, relay, cols, part, landed, handed, placed, last, late, direct,
                   b_send, b_recv, b_own, a_send, a_recv, y_send, y_recv, p_send, p_recv,
-                  r_send, r_recv, l_send, l_recv, o_send, o_recv, d_send, d_recv, ready):
+                  r_send, r_recv, l_send, l_recv, o_send, o_recv, d_send, d_recv, late_recv, ready):
     r, w = lax.axis_index("rep"), lax.axis_index("wide")
     up, down, across = (r + 1) % reps, (r + reps - 1) % reps, (r + 2) % reps
     groups = members // GROUP
@@ -86,7 +86,7 @@
     near = pl.ds(0, GROUP)
     far_planes = (2, 1, 3)
     far_pieces = tuple(pl.ds((k + 1) * GROUP, GROUP) for k in range(3))
-    stretches = (pl.ds(0, depth // 2), pl.ds(depth // 2, depth // 2))
+    stretches = pl.ds(0, depth * 7 // 10), pl.ds(depth * 7 // 10, depth * 3 // 10)
 
     def send_columns(half):
         remote(integ.at[irrep(3, half)], cols.at[half, 0, theirs], b_send.at[half, 0], b_recv.at[half, 0], up, w).start()
@@ -172,7 +172,7 @@
     def multiply_near(role, stretch):
         inner = stretches[stretch]
         wait_for(rows.at[1, role, 3, near, :, inner], p_recv.at[role, 3 + stretch])
-        left = rows[1, role, 3, near, :, inner].reshape(GROUP * owned, depth // 2)
+        left = rows[1, role, 3, near, :, inner].reshape(GROUP * owned, inner.size)
         some = lax.dot_general(
             left, cols[1, role, :, inner], (((1,), (1,)), ((), ())), preferred_element_type=jnp.float32
         ).reshape(GROUP, owned, 2 * cuts)
@@ -217,23 +217,21 @@
     def add_up(half, stage):
         slots = stages[stage]
         wait_for(landed.at[half, :, :, slots], r_recv.at[half, stage])
-        summed[half, :, slots] = jnp.sum(landed[half, :, :, slots], axis=1)
-        hand_out(half, ((0, 1), (2,), (3,))[stage])
+        handed[half, :, slots] = jnp.sum(landed[half, :, :, slots], axis=1).astype(handed.dtype)
+        for role in range(2):
+            g = irrep(role, half)
+            for slot in ((0, 1), (2,), (3,))[stage]:
+                if slot == 0:
+                    placed[g, role] = handed[half, role, 0]
+                else:
+                    remote(handed.at[half, role, slot], placed.at[g, role], o_send.at[half, role, slot - 1],
+                           o_recv.at[half], beside[slot][role], w).start()
 
     def add_up_far():
         wait_for(landed.at[1, :, pl.ds(GROUP, 2 * GROUP), 3], l_recv)
-        summed[1, :, 3] = jnp.sum(landed[1, :, pl.ds(GROUP, 2 * GROUP), 3], axis=1)
-        hand_out(1, (3,))
-
-    def hand_out(half, slots):
-        for role in range(2):
-            g = irrep(role, half)
-            for slot in slots:
-                if slot == 0:
-                    placed[g, role] = summed[half, role, 0]
-                else:
-                    remote(summed.at[half, role, slot], placed.at[g, role], o_send.at[half, role, slot - 1],
-                           o_recv.at[half], beside[slot][role], w).start()
+        last[...] = jnp.sum(landed[1, :, pl.ds(GROUP, 2 * GROUP), 3], axis=1)
+        for role in range(2):
+            remote(last.at[role], late.at[role], o_send.at[1, role, 2], late_recv.at[role], beside[3][role], w).start()
 
     def finish(half):
         for p in range(reps):
@@ -241,8 +239,9 @@
             found = {}
             for role, beyond in ((0, reps - 1), (1, 1)):
                 here = (p + role) % reps
-                found[here] = placed[g, role, :, :cuts]
-                found[(here + beyond) % reps] = placed[g, role, :, cuts:]
+                piece = placed[g, role].astype(jnp.float32)
+                found[here] = piece[:, :cuts]
+                found[(here + beyond) % reps] = piece[:, cuts:]
             out[g] = jnp.concatenate([found[q] for q in range(reps)], axis=1).astype(out.dtype)
 
     send_columns(0)
@@ -332,19 +331,19 @@
         for index in range(2):
             wait_for(rows.at[1, role, 0, near, :, stretches[index]], p_send.at[role, 3 + index])
         for slot in range(3):
-            wait_for(summed.at[0, role, slot], o_send.at[0, role, slot])
+            wait_for(handed.at[0, role, slot], o_send.at[0, role, slot])
         for slot in range(2):
-            wait_for(summed.at[1, role, slot], o_send.at[1, role, slot])
+            wait_for(handed.at[1, role, slot], o_send.at[1, role, slot])
     wait_for(landed.at[1, :, some, stages[1]], r_send.at[1, 1])
     wait_for(landed.at[1, :, pl.ds(GROUP, 2 * GROUP), 3], l_send)
     for role in range(2):
         wait_for(direct.at[role], d_send.at[role])
         wait_for(direct.at[role], d_recv.at[role])
-        wait_for(summed.at[1, role, 2], o_send.at[1, role, 2])
-    wait_for(placed.at[pl.ds(reps, reps - 1)], o_recv.at[1])
+        wait_for(last.at[role], o_send.at[1, role, 2])
+    wait_for(placed.at[pl.ds(reps, reps - 2)], o_recv.at[1])
     for role, behind in ((0, 1), (1, 0)):
-        g = irrep(behind, 1)
-        placed[g, role] = placed[g, role] + jnp.sum(direct[role], axis=(0, 1))
+        wait_for(late.at[role], late_recv.at[role])
+        placed[irrep(behind, 1), role] = (late[role] + jnp.sum(direct[role], axis=(0, 1))).astype(placed.dtype)
     finish(1)
 
 
@@ -365,8 +364,10 @@
             pltpu.VMEM((halves, 2, 2 * cuts, depth), bf16),
             pltpu.VMEM((halves, 2, members, 4, owned, 2 * cuts), f32),
             pltpu.VMEM((halves, 2, members, 4, owned, 2 * cuts), f32),
-            pltpu.VMEM((halves, 2, 4, owned, 2 * cuts), f32),
-            pltpu.VMEM((irreps, 2, owned, 2 * cuts), f32),
+            pltpu.VMEM((halves, 2, 4, owned, 2 * cuts), bf16),
+            pltpu.VMEM((irreps, 2, owned, 2 * cuts), bf16),
+            pltpu.VMEM((2, owned, 2 * cuts), f32),
+            pltpu.VMEM((2, owned, 2 * cuts), f32),
             pltpu.VMEM((2, 2, GROUP, owned, 2 * cuts), f32),
             dma((halves, 2)), dma((halves, 2)), dma((halves, 2)),
             dma((halves, 4)), dma((halves, 4)),
@@ -375,7 +376,7 @@
             dma((halves, 3)), dma((halves, 3)),
             dma, dma,
             dma((halves, 2, 3)), dma((halves,)),
-            dma((2,)), dma((2,)), pltpu.SemaphoreType.REGULAR((2,)),
+            dma((2,)), dma((2,)), dma((2,)), pltpu.SemaphoreType.REGULAR((2,)),
         ],
         compiler_params=pltpu.CompilerParams(collective_id=0, has_side_effects=True, vmem_limit_bytes=52 * MIB),
         cost_estimate=pl.CostEstimate(

time: 142 us -> 142 us (level)
  no operation moved by 1% of the time
where the time goes in v8:
time: 142 us
  Pallas kernels  141 us (99%)
    pallas_call x1, Pallas kernels, per_device(): pl.pallas_call(functools.partial(ladder_kernel, reps, members), out_shape...  141 us

profile of v8, /device:TPU:1, one launch (start us, length us, event | category | flops | bytes accessed | tf_op | source)
XLA Modules:
  0.0 141.9 jit_solution(6483392704459308296)
XLA Ops:
  0.0 0.0 copy-start
  0.0 141.1 %ladder.1 = bf16[8,4,768]{2,1,0:T(4,128)(2,1)S(1)} custom-call(bf16[8,32,4,2560]{3,2,1,0:T(4,128)(2,1)} %amp.1, bf16[8,192,2560]{2,1,0:T(8,128)(2,1)} %integ.1), custom_call_target="tpu_custom_call" | custom-call | flops 4026531840 | bytes 27262976 | tf_op jit(solution)/shard_map/ladder/pallas_call | solution.py:356
  141.2 0.0 copy-done
  141.2 0.7 compare_select_fusion
  (1 shorter events, 0.0 us)
Async XLA Ops:
  0.0 141.2 %copy-start = (s32[8]{0:T(128)S(1)}, s32[8]{0:T(128)}, u32[]{:S(2)}) copy-start(s32[8]{0:T(128)} %param.5) | copy-start | bytes 100

commit v9 on v8

--- a/solution.py
+++ b/solution.py
@@ -320,10 +320,10 @@
     for role in range(2):
         multiply_near(role, 1)
         give_direct(role, 0, 0, 0)
+    add_up_far()
     add_up(1, 1)
     wait_for(placed.at[pl.ds(0, reps - 1)], o_recv.at[0])
     finish(0)
-    add_up_far()
     for role in range(2):
         wait_for(rows.at[1, role, 0], y_send.at[1, role, 1])
         for index in range(3):

time: 142 us -> 142 us (level)
  no operation moved by 1% of the time
where the time goes in v9:
time: 142 us
  Pallas kernels  141 us (99%)
    pallas_call x1, Pallas kernels, per_device(): pl.pallas_call(functools.partial(ladder_kernel, reps, members), out_shape...  141 us

profile of v9, /device:TPU:1, one launch (start us, length us, event | category | flops | bytes accessed | tf_op | source)
XLA Modules:
  0.0 141.9 jit_solution(16353250759571347712)
XLA Ops:
  0.0 0.0 copy-start
  0.0 141.1 %ladder.1 = bf16[8,4,768]{2,1,0:T(4,128)(2,1)S(1)} custom-call(bf16[8,32,4,2560]{3,2,1,0:T(4,128)(2,1)} %amp.1, bf16[8,192,2560]{2,1,0:T(8,128)(2,1)} %integ.1), custom_call_target="tpu_custom_call" | custom-call | flops 4026531840 | bytes 27262976 | tf_op jit(solution)/shard_map/ladder/pallas_call | solution.py:356
  141.2 0.0 copy-done
  141.2 0.7 compare_select_fusion
  (1 shorter events, 0.0 us)
Async XLA Ops:
  0.0 141.2 %copy-start = (s32[8]{0:T(128)S(1)}, s32[8]{0:T(128)}, u32[]{:S(2)}) copy-start(s32[8]{0:T(128)} %param.5) | copy-start | bytes 100
